TPU v7x, 128 devices: a whole 4x4x4 slice. The times are simulated.
128 devices in a mesh: row: 16 (over z, y), col: 8 (over x, core).
Axes of the slice: x: 4, y: 4, z: 4, core: 2. Of those that a mesh axis runs over, the one named last changes fastest.
Arguments:
- image: bfloat16 [64, 64, 6144], P('row', None, 'col'), may hold values from -8 to 8
- filter_bank: float32 [2, 64, 64, 6144], P(None, None, 'row', 'col'), may hold values from -6 to 6
- gain_first: float32 [6144], P('col'), may hold values from 0.1 to 1.9
- gain_second: float32 [6144], P('col'), may hold values from 0.1 to 1.9
- w_in: bfloat16 [6144, 24576], P('col', 'row'), may hold values from -0.078125 to 0.078125
- b_in: float32 [24576], P('row'), may hold values from -4 to 4
- w_out: bfloat16 [24576, 6144], P('row', 'col'), may hold values from -0.0390625 to 0.0390625
- b_out: float32 [6144], P('col'), may hold values from -3 to 3
Outputs:
- block_out: bfloat16 [64, 64, 6144], P('row', None, 'col')
All inputs are finite; a program needn't handle non-finite values.
Results may differ from a plain program's by a relative error of at most 0.017.
Values may be sent and summed in bfloat16 or wider, within the bound.
No kernel may reach another device: no remote copies, remote signals or barrier semaphores. Data moves between devices by JAX's collectives and lax.ppermute only.
A program may use at most 128 MiB of HBM per device.

v0:
```python
import math
import jax
import jax.numpy as jnp
from jax import lax
from jax.sharding import PartitionSpec as P


def tables(count):
    index = jnp.arange(count, dtype=jnp.int32)
    angle = (index[:, None] * index[None, :] % count).astype(jnp.float32) * (2.0 * math.pi / count)
    return (jnp.cos(angle), jnp.sin(angle))


def finish_norm(values, totals, width_all):
    mean = totals[0][..., None] / width_all
    square = totals[1][..., None] / width_all
    return (values - mean) / jnp.sqrt(square - mean * mean + 1e-05)


def on_device(image, filter_bank, gain_first, gain_second, w_in, b_in, w_out, b_out):
    high = lax.Precision.HIGHEST
    rows_here, width, chans = image.shape
    height = rows_here * lax.axis_size("row")
    width_all = chans * lax.axis_size("col")
    source = image.astype(jnp.float32)
    totals = lax.psum((jnp.sum(source, axis=-1), jnp.sum(source * source, axis=-1)), "col")
    normed = finish_norm(source, totals, width_all) * gain_first
    cos_w, sin_w = tables(width)
    cos_h, sin_h = tables(height)
    col_re = jnp.einsum("rcd,ck->rkd", normed, cos_w, precision=high)
    col_im = -jnp.einsum("rcd,ck->rkd", normed, sin_w, precision=high)
    col_re, col_im = (
        lax.all_to_all(
            col_re.astype(jnp.bfloat16), "row", split_axis=1, concat_axis=0, tiled=True
        ).astype(col_re.dtype),
        lax.all_to_all(
            col_im.astype(jnp.bfloat16), "row", split_axis=1, concat_axis=0, tiled=True
        ).astype(col_im.dtype),
    )
    spec_re = jnp.einsum("rn,rkd->nkd", cos_h, col_re, precision=high) + jnp.einsum(
        "rn,rkd->nkd", sin_h, col_im, precision=high
    )
    spec_im = jnp.einsum("rn,rkd->nkd", cos_h, col_im, precision=high) - jnp.einsum(
        "rn,rkd->nkd", sin_h, col_re, precision=high
    )
    filt_re = filter_bank[0] * spec_re - filter_bank[1] * spec_im
    filt_im = filter_bank[0] * spec_im + filter_bank[1] * spec_re
    back_re = jnp.einsum("nr,nkd->rkd", cos_h, filt_re, precision=high) - jnp.einsum(
        "nr,nkd->rkd", sin_h, filt_im, precision=high
    )
    back_im = jnp.einsum("nr,nkd->rkd", sin_h, filt_re, precision=high) + jnp.einsum(
        "nr,nkd->rkd", cos_h, filt_im, precision=high
    )
    back_re, back_im = (
        lax.all_to_all(
            back_re.astype(jnp.bfloat16), "row", split_axis=0, concat_axis=1, tiled=True
        ).astype(back_re.dtype),
        lax.all_to_all(
            back_im.astype(jnp.bfloat16), "row", split_axis=0, concat_axis=1, tiled=True
        ).astype(back_im.dtype),
    )
    mixed = (
        jnp.einsum("rkd,kc->rcd", back_re, cos_w, precision=high)
        - jnp.einsum("rkd,kc->rcd", back_im, sin_w, precision=high)
    ) / (height * width)
    resid = (source + mixed).reshape(rows_here * width, chans)
    totals_two = lax.psum((jnp.sum(resid, axis=-1), jnp.sum(resid * resid, axis=-1)), "col")
    act = (finish_norm(resid, totals_two, width_all) * gain_second).astype(jnp.bfloat16)
    partial_pre = jnp.dot(
        lax.all_gather(act, "row", axis=0, tiled=True), w_in, preferred_element_type=jnp.float32
    )
    summed = lax.psum_scatter(
        partial_pre.astype(jnp.bfloat16), "col", scatter_dimension=0, tiled=True
    ).astype(jnp.float32)
    hidden = jax.nn.gelu(summed + b_in, approximate=False).astype(jnp.bfloat16)
    partial_out = jnp.dot(
        lax.all_gather(hidden, "col", axis=0, tiled=True), w_out, preferred_element_type=jnp.float32
    )
    proj = lax.psum_scatter(
        partial_out.astype(jnp.bfloat16), "row", scatter_dimension=0, tiled=True
    ).astype(jnp.float32)
    result = (resid + proj + b_out).astype(jnp.bfloat16)
    return result.reshape(rows_here, width, chans)


def solution(mesh):
    placed = (
        P("row", None, "col"),
        P(None, None, "row", "col"),
        P("col"),
        P("col"),
        P("col", "row"),
        P("row"),
        P("row", "col"),
        P("col"),
    )
    return jax.shard_map(
        on_device, mesh=mesh, in_specs=placed, out_specs=P("row", None, "col"), check_vma=False
    )
```

profile of v0, /device:TPU:0, one launch (start us, length us, event | category | flops | bytes accessed | tf_op | source)
XLA Modules:
  0.0 433.0 jit_solution(3554515615974507233)
XLA Ops:
  6.5 0.0 copy-start
  6.5 1.3 convert_reduce_fusion
  7.9 14.7 %all-reduce.1 = (f32[4,64]{1,0:T(4,128)S(1)}, f32[4,64]{1,0:T(4,128)S(1)}) all-reduce(f32[4,64]{1,0:T(4,128)S(1)} %get-tuple-element.8, f32[4,64]{1,0:T(4,128)S(1)} %get-tuple-element.7), channel_id=1, replica_groups=mesh['row'=16,'col'=8] {'col'}, use_global_device_ids=true, to_apply=%region_3.0 | all-reduce | flops 512 | bytes 4096 | tf_op jit(solution)/shard_map/psum | solution.py:26
  22.6 2.0 fusion.19
  24.6 1.1 copy.18
  25.6 8.0 %all-to-all-start.1 = ((bf16[4,64,768]{2,0,1:T(4,128)(2,1)}), bf16[4,64,768]{2,0,1:T(4,128)(2,1)S(1)}, u32[]{:S(2)}, u32[]{:S(2)}) async-start(bf16[4,64,768]{2,0,1:T(4,128)(2,1)} %copy.18), calls=%async_computation.1 | async-start | bytes 786432 | tf_op jit(solution)/shard_map/all_to_all | solution.py:36
  33.7 1.0 fusion.18
  34.7 1.1 copy.16
  35.7 7.3 %all-to-all-done.1 = bf16[4,64,768]{2,0,1:T(4,128)(2,1)S(1)} async-done(((bf16[4,64,768]{2,0,1:T(4,128)(2,1)}), bf16[4,64,768]{2,0,1:T(4,128)(2,1)S(1)}, u32[]{:S(2)}, u32[]{:S(2)}) %all-to-all-start.1) | async-done | bytes 393248 | tf_op jit(solution)/shard_map/all_to_all | solution.py:36
  43.1 3.6 all-to-all-start
  46.6 2.6 fusion.122
  49.3 0.9 copy.43
  50.2 1.1 all_to_all.59
  51.2 4.7 %all-to-all-done = bf16[4,64,768]{2,0,1:T(4,128)(2,1)S(1)} async-done(((bf16[4,64,768]{2,0,1:T(4,128)(2,1)}), bf16[4,64,768]{2,0,1:T(4,128)(2,1)S(1)}, u32[]{:S(2)}, u32[]{:S(2)}) %all-to-all-start) | async-done | bytes 393248 | tf_op jit(solution)/shard_map/all_to_all | solution.py:33
  56.0 0.9 copy.44
  56.9 1.1 all_to_all.55
  58.0 0.6 fusion.53
  58.6 0.6 fusion.51
  59.2 0.6 convolution_subtract_fusion.2
  59.7 0.0 copy-done.2
  59.8 0.0 copy-done.3
  59.8 0.9 multiply_add_fusion
  60.6 0.0 copy-start.1
  60.7 0.9 fusion.49
  61.6 0.0 copy-done.1
  61.6 0.9 fusion.15
  62.5 1.1 copy.21
  63.6 3.6 all-to-all-start.2
  67.2 0.9 fusion.40
  68.1 2.0 fusion.16
  70.2 0.0 copy-start.5
  70.2 1.1 copy.23
  71.2 5.3 %all-to-all-done.2 = bf16[64,4,768]{2,1,0:T(4,128)(2,1)S(1)} async-done(((bf16[64,4,768]{2,1,0:T(4,128)(2,1)}), bf16[64,4,768]{2,1,0:T(4,128)(2,1)S(1)}, u32[]{:S(2)}, u32[]{:S(2)}) %all-to-all-start.2) | async-done | bytes 393248 | tf_op jit(solution)/shard_map/all_to_all | solution.py:55
  76.5 3.6 all-to-all-start.3
  80.1 0.2 all-gather.3.cloned.1.call-start
  80.3 0.9 copy.42
  81.2 1.8 all_to_all.63
  83.0 6.4 %all-to-all-done.3 = bf16[64,4,768]{2,1,0:T(4,128)(2,1)S(1)} async-done(((bf16[64,4,768]{2,1,0:T(4,128)(2,1)}), bf16[64,4,768]{2,1,0:T(4,128)(2,1)S(1)}, u32[]{:S(2)}, u32[]{:S(2)}) %all-to-all-start.3) | async-done | bytes 393248 | tf_op jit(solution)/shard_map/all_to_all | solution.py:58
  89.4 0.1 copy.41
  89.6 0.8 all_to_all.67
  90.4 1.6 fusion.47
  92.0 0.0 copy-done.5
  92.0 1.8 fusion.121
  93.8 0.1 reduce_sum.43
  93.9 0.1 reduce_sum.45
  94.0 12.4 %all-reduce = (f32[256]{0:T(256)S(1)}, f32[256]{0:T(256)S(1)}) all-reduce(f32[256]{0:T(256)S(1)} %reduce_sum.45, f32[256]{0:T(256)S(1)} %reduce_sum.43), channel_id=1, replica_groups=mesh['row'=16,'col'=8] {'col'}, use_global_device_ids=true, to_apply=%region_7.8 | all-reduce | flops 512 | bytes 4096 | tf_op jit(solution)/shard_map/psum | solution.py:67
  106.4 0.9 fusion.25
  107.3 0.0 all-gather.3.cloned.1.call-update
  107.3 0.0 reduce-scatter.3.cloned.1.call-start
  107.4 56.5 %all-gather.3.cloned.1.call-done = bf16[4096,768]{1,0:T(8,128)(2,1)} async-done(((bf16[256,768]{1,0:T(8,128)(2,1)}), bf16[4096,768]{1,0:T(8,128)(2,1)}) %all-gather.3.cloned.1.call-update) | async-done | bytes 6291472 | tf_op jit(solution)/shard_map/all_gather | solution.py:70
  163.9 15.2 %convolution_convert_fusion = bf16[4096,1536]{1,0:T(8,128)(2,1)} fusion(bf16[4096,768]{1,0:T(8,128)(2,1)} %all-gather.3.cloned.1.call-done, bf16[768,1536]{1,0:T(8,128)(2,1)S(1)} %copy-done), kind=kOutput, calls=%fused_computation | convolution fusion | flops 9669967872 | bytes 21233664 | tf_op jit(solution)/shard_map/dot_general | solution.py:69
  179.1 0.0 reduce-scatter.3.cloned.1.call-update
  179.1 0.0 all-gather.5.cloned.1.call-start
  179.1 72.0 %reduce-scatter.3.cloned.1.call-done = bf16[512,1536]{1,0:T(8,128)(2,1)} async-done(((bf16[4096,1536]{1,0:T(8,128)(2,1)}), bf16[512,1536]{1,0:T(8,128)(2,1)}) %reduce-scatter.3.cloned.1.call-update) | async-done | bytes 1572880 | tf_op jit(solution)/shard_map/reduce_scatter | solution.py:72
  251.2 0.0 copy-done.6
  251.2 8.9 %fusion.2 = bf16[512,1536]{1,0:T(8,128)(2,1)} fusion(bf16[512,1536]{1,0:T(8,128)(2,1)} %reduce-scatter.3.cloned.1.call-done, f32[1536]{0:T(1024)S(1)} %copy-done.6), kind=kLoop, calls=%fused_computation.5 | loop fusion | flops 52690944 | bytes 3151872 | tf_op jit(solution)/shard_map/convert_element_type | solution.py:75
  260.0 0.0 all-gather.5.cloned.1.call-update
  260.1 0.0 reduce-scatter.5.cloned.1.call-start
  260.1 67.0 %all-gather.5.cloned.1.call-done = bf16[4096,1536]{1,0:T(8,128)(2,1)} async-done(((bf16[512,1536]{1,0:T(8,128)(2,1)}), bf16[4096,1536]{1,0:T(8,128)(2,1)}) %all-gather.5.cloned.1.call-update) | async-done | bytes 12582928 | tf_op jit(solution)/shard_map/all_gather | solution.py:77
  327.1 15.3 %convolution_convert_fusion.1 = bf16[4096,768]{1,0:T(8,128)(2,1)} fusion(bf16[4096,1536]{1,0:T(8,128)(2,1)} %all-gather.5.cloned.1.call-done, bf16[1536,768]{1,0:T(8,128)(2,1)} %param.14), kind=kOutput, calls=%fused_computation.1 | convolution fusion | flops 9666822144 | bytes 21233664 | tf_op jit(solution)/shard_map/dot_general | solution.py:76
  342.4 0.0 reduce-scatter.5.cloned.1.call-update
  342.5 82.1 %reduce-scatter.5.cloned.1.call-done = bf16[256,768]{1,0:T(8,128)(2,1)} async-done(((bf16[4096,768]{1,0:T(8,128)(2,1)}), bf16[256,768]{1,0:T(8,128)(2,1)}) %reduce-scatter.5.cloned.1.call-update) | async-done | bytes 393232 | tf_op jit(solution)/shard_map/reduce_scatter | solution.py:79
  424.6 0.0 copy-done.8
  424.6 1.9 fusion.27
  (13 shorter events, 0.0 us)
Async XLA Ops:
  6.5 157.3 %copy-start = (bf16[768,1536]{1,0:T(8,128)(2,1)S(1)}, bf16[768,1536]{1,0:T(8,128)(2,1)}, u32[]{:S(2)}) copy-start(bf16[768,1536]{1,0:T(8,128)(2,1)} %param.12) | copy-start | bytes 7077892
  6.5 27.1 %copy-start.4 = (bf16[4,64,768]{2,1,0:T(8,128)(2,1)S(1)}, bf16[4,64,768]{2,1,0:T(8,128)(2,1)}, u32[]{:S(2)}) copy-start(bf16[4,64,768]{2,1,0:T(8,128)(2,1)} %param.8) | copy-start | bytes 1179652
  6.5 27.1 %copy-start.9 = (f32[768]{0:T(1024)S(1)}, f32[768]{0:T(1024)}, u32[]{:S(2)}) copy-start(f32[768]{0:T(1024)} %param.10) | copy-start | bytes 9220
  25.6 17.4 %all-to-all-start.1 = ((bf16[4,64,768]{2,0,1:T(4,128)(2,1)}), bf16[4,64,768]{2,0,1:T(4,128)(2,1)S(1)}, u32[]{:S(2)}, u32[]{:S(2)}) async-start(bf16[4,64,768]{2,0,1:T(4,128)(2,1)} %copy.18), calls=%async_computation.1 | async-start | bytes 786432 | tf_op jit(solution)/shard_map/all_to_all | solution.py:36
  43.1 12.9 %all-to-all-start = ((bf16[4,64,768]{2,0,1:T(4,128)(2,1)}), bf16[4,64,768]{2,0,1:T(4,128)(2,1)S(1)}, u32[]{:S(2)}, u32[]{:S(2)}) async-start(bf16[4,64,768]{2,0,1:T(4,128)(2,1)} %copy.16), calls=%async_computation | async-start | bytes 786432 | tf_op jit(solution)/shard_map/all_to_all | solution.py:33
  58.0 1.8 copy-start.2
  58.0 1.8 copy-start.3
  60.6 0.9 copy-start.1
  63.6 12.9 %all-to-all-start.2 = ((bf16[64,4,768]{2,1,0:T(4,128)(2,1)}), bf16[64,4,768]{2,1,0:T(4,128)(2,1)S(1)}, u32[]{:S(2)}, u32[]{:S(2)}) async-start(bf16[64,4,768]{2,1,0:T(4,128)(2,1)} %copy.21), calls=%async_computation.2 | async-start | bytes 786432 | tf_op jit(solution)/shard_map/all_to_all | solution.py:55
  70.2 21.8 %copy-start.5 = (bf16[4,64,768]{2,1,0:T(8,128)(2,1)S(1)}, bf16[4,64,768]{2,1,0:T(8,128)(2,1)}, u32[]{:S(2)}) copy-start(bf16[4,64,768]{2,1,0:T(8,128)(2,1)} %param.8) | copy-start | bytes 1179652
  76.5 12.9 %all-to-all-start.3 = ((bf16[64,4,768]{2,1,0:T(4,128)(2,1)}), bf16[64,4,768]{2,1,0:T(4,128)(2,1)S(1)}, u32[]{:S(2)}, u32[]{:S(2)}) async-start(bf16[64,4,768]{2,1,0:T(4,128)(2,1)} %copy.23), calls=%async_computation.3 | async-start | bytes 786432 | tf_op jit(solution)/shard_map/all_to_all | solution.py:58
  80.1 83.8 %all-gather.3.cloned.1.call-start = ((), (), s32[]{:S(2)}) async-start(), calls=%async_computation.6 | async-start | bytes 6684672 | tf_op jit(solution)/shard_map/all_gather | solution.py:70
  81.2 25.2 %copy-start.7 = (f32[768]{0:T(1024)S(1)}, f32[768]{0:T(1024)}, u32[]{:S(2)}) copy-start(f32[768]{0:T(1024)} %param.11) | copy-start | bytes 9220
  107.3 143.8 %reduce-scatter.3.cloned.1.call-start = ((), (), s32[]{:S(2)}) async-start(), calls=%async_computation.7 | async-start | bytes 14155776 | tf_op jit(solution)/shard_map/reduce_scatter | solution.py:72
  179.1 72.1 %copy-start.6 = (f32[1536]{0:T(1024)S(1)}, f32[1536]{0:T(1024)}, u32[]{:S(2)}) copy-start(f32[1536]{0:T(1024)} %param.13) | copy-start | bytes 18436
  179.1 148.1 %all-gather.5.cloned.1.call-start = ((), (), s32[]{:S(2)}) async-start(), calls=%async_computation.8 | async-start | bytes 14155776 | tf_op jit(solution)/shard_map/all_gather | solution.py:77
  260.1 164.5 %reduce-scatter.5.cloned.1.call-start = ((), (), s32[]{:S(2)}) async-start(), calls=%async_computation.9 | async-start | bytes 6684672 | tf_op jit(solution)/shard_map/reduce_scatter | solution.py:79
  342.4 82.1 %copy-start.8 = (f32[768]{0:T(1024)S(1)}, f32[768]{0:T(1024)}, u32[]{:S(2)}) copy-start(f32[768]{0:T(1024)} %param.15) | copy-start | bytes 9220
Sparse Core Ops, SparseCore 0:
  107.5 56.3 all-gather.2
  179.2 71.9 reduce-scatter.2
  260.2 66.9 all-gather.4
  342.6 81.9 reduce-scatter.4
where the time goes:
time: 434 us; the launch traced here: 433 us
  waiting for transfers between devices  301 us (69%)
  matrix products  44.3 us (10%)
  blocking collectives  27.1 us (6%)
  starting transfers between devices  19.1 us (4%)
  local copies, waits for them, and re-layouts  14.7 us (3%)
  between operations  13.4 us (3%)
  other arithmetic  13 us (3%)
    reduce_scatter x1, waiting for transfers between devices, on_device(): lax.psum_scatter(partial_out.astype(jnp.bfloat16), 'row', scatter_dimensi...  82.1 us
    reduce_scatter x1, waiting for transfers between devices, on_device(): lax.psum_scatter(partial_pre.astype(jnp.bfloat16), 'col', scatter_dimensi...  72 us
    all_gather x1, waiting for transfers between devices, on_device(): lax.all_gather(hidden, 'col', axis=0, tiled=True)  67 us
    all_gather x1, waiting for transfers between devices, on_device(): lax.all_gather(act, 'row', axis=0, tiled=True)  56.5 us
    dot_general x1, matrix products, on_device(): jnp.dot(lax.all_gather(hidden, 'col', axis=0, tiled=True), w_out, preferr...  15.3 us
    dot_general x1, matrix products, on_device(): jnp.dot(lax.all_gather(act, 'row', axis=0, tiled=True), w_in, preferred_e...  15.2 us
    psum x1, blocking collectives, on_device(): lax.psum((jnp.sum(source, axis=-1), jnp.sum(source * source, axis=-1)), '...  14.7 us
    psum x1, blocking collectives, on_device(): lax.psum((jnp.sum(resid, axis=-1), jnp.sum(resid * resid, axis=-1)), 'col')  12.4 us
  transfers between devices with their start and end apart: 8, of which 8 were waited for; matrix products, arithmetic and copies ran while one was open for 2% of the time, Pallas kernels for 0%

commit v1 on v0

--- a/solution.py
+++ b/solution.py
@@ -73,8 +73,15 @@
         partial_pre.astype(jnp.bfloat16), "col", scatter_dimension=0, tiled=True
     ).astype(jnp.float32)
     hidden = jax.nn.gelu(summed + b_in, approximate=False).astype(jnp.bfloat16)
+
+    def do_stacks_all_in(block_here, shard_axis, which_dim):
+        new = jnp.stack([block_here for _ in range(jax.lax.psum(1, shard_axis))])
+        kept_arr = jax.lax.all_to_all(new, axis_name=shard_axis, split_axis=0, concat_axis=0)
+        long_array = jnp.concatenate(kept_arr, axis=which_dim)
+        return long_array
+
     partial_out = jnp.dot(
-        lax.all_gather(hidden, "col", axis=0, tiled=True), w_out, preferred_element_type=jnp.float32
+        do_stacks_all_in(hidden, "col", 0), w_out, preferred_element_type=jnp.float32
     )
     proj = lax.psum_scatter(
         partial_out.astype(jnp.bfloat16), "row", scatter_dimension=0, tiled=True

time: 434 us -> 513 us (1.18)
  blocking collectives: 27.1 us -> 173 us
  waiting for transfers between devices: 301 us -> 233 us
  local copies, waits for them, and re-layouts: 14.7 us -> 20.3 us
    all_to_all x0 -> x1, blocking collectives: none -> 146 us  [do_stacks_all_in(): jax.lax.all_to_all(new, axis_name=shard_axis, split_axis=0, concat_axis=0)]
    all_gather x1 -> x0, waiting for transfers between devices: 67 us -> none  [on_device(): lax.all_gather(hidden, 'col', axis=0, tiled=True)]
    another operation x0 -> x1, local copies, waits for them, and re-layouts: none -> 5.6 us  [do_stacks_all_in(): new = jnp.stack([block_here for _ in range(jax.lax.psum(1, shard_axis))])]
  transfers between devices with their start and end apart: 8 -> 7, of which waited for: 8 -> 7; matrix products, arithmetic and copies ran while one was open for 2% -> 2% of each run, Pallas kernels for 0% -> 0%
where the time goes in v1:
time: 513 us; the launch traced here: 512 us
  waiting for transfers between devices  233 us (45%)
  blocking collectives  173 us (34%)
  matrix products  40.8 us (8%)
  local copies, waits for them, and re-layouts  20.3 us (4%)
  starting transfers between devices  19 us (4%)
  between operations  13.4 us (3%)
  other arithmetic  12.2 us (2%)
    all_to_all x1, blocking collectives, do_stacks_all_in(): jax.lax.all_to_all(new, axis_name=shard_axis, split_axis=0, concat_axis=0)  146 us
    reduce_scatter x1, waiting for transfers between devices, on_device(): lax.psum_scatter(partial_out.astype(jnp.bfloat16), 'row', scatter_dimensi...  81 us
    reduce_scatter x1, waiting for transfers between devices, on_device(): lax.psum_scatter(partial_pre.astype(jnp.bfloat16), 'col', scatter_dimensi...  72 us
    all_gather x1, waiting for transfers between devices, on_device(): lax.all_gather(act, 'row', axis=0, tiled=True)  56.5 us
    dot_general x1, matrix products, on_device(): jnp.dot(lax.all_gather(act, 'row', axis=0, tiled=True), w_in, preferred_e...  15.2 us
    psum x1, blocking collectives, on_device(): lax.psum((jnp.sum(source, axis=-1), jnp.sum(source * source, axis=-1)), '...  14.7 us
    psum x1, blocking collectives, on_device(): lax.psum((jnp.sum(resid, axis=-1), jnp.sum(resid * resid, axis=-1)), 'col')  12.4 us
    dot_general x1, matrix products, on_device(): jnp.dot(do_stacks_all_in(hidden, 'col', 0), w_out, preferred_element_type...  11.7 us
  transfers between devices with their start and end apart: 7, of which 7 were waited for; matrix products, arithmetic and copies ran while one was open for 2% of the time, Pallas kernels for 0%

profile of v1, /device:TPU:0, one launch (start us, length us, event | category | flops | bytes accessed | tf_op | source)
XLA Modules:
  0.0 511.7 jit_solution(9821385349188641867)
XLA Ops:
  6.5 0.0 copy-start
  6.5 1.3 convert_reduce_fusion
  7.9 14.7 %all-reduce.1 = (f32[4,64]{1,0:T(4,128)S(1)}, f32[4,64]{1,0:T(4,128)S(1)}) all-reduce(f32[4,64]{1,0:T(4,128)S(1)} %get-tuple-element.8, f32[4,64]{1,0:T(4,128)S(1)} %get-tuple-element.7), channel_id=1, replica_groups=mesh['row'=16,'col'=8] {'col'}, use_global_device_ids=true, to_apply=%region_3.0 | all-reduce | flops 512 | bytes 4096 | tf_op jit(solution)/shard_map/psum | solution.py:26
  22.6 2.0 fusion.19
  24.6 1.1 copy.18
  25.6 8.0 %all-to-all-start.1 = ((bf16[4,64,768]{2,0,1:T(4,128)(2,1)}), bf16[4,64,768]{2,0,1:T(4,128)(2,1)S(1)}, u32[]{:S(2)}, u32[]{:S(2)}) async-start(bf16[4,64,768]{2,0,1:T(4,128)(2,1)} %copy.18), calls=%async_computation.1 | async-start | bytes 786432 | tf_op jit(solution)/shard_map/all_to_all | solution.py:36
  33.7 0.0 copy-done.5
  33.7 0.0 copy-done.11
  33.7 1.0 fusion.18
  34.7 1.0 copy.16
  35.7 7.3 %all-to-all-done.1 = bf16[4,64,768]{2,0,1:T(4,128)(2,1)S(1)} async-done(((bf16[4,64,768]{2,0,1:T(4,128)(2,1)}), bf16[4,64,768]{2,0,1:T(4,128)(2,1)S(1)}, u32[]{:S(2)}, u32[]{:S(2)}) %all-to-all-start.1) | async-done | bytes 393248 | tf_op jit(solution)/shard_map/all_to_all | solution.py:36
  43.1 3.6 all-to-all-start
  46.6 2.6 fusion.122
  49.3 0.9 copy.43
  50.1 1.1 all_to_all.62
  51.2 4.7 all-to-all-done
  56.0 0.9 copy.44
  56.9 1.1 all_to_all.58
  58.0 0.0 copy-start.3
  58.0 0.6 fusion.53
  58.6 0.6 fusion.51
  59.2 0.6 convolution_subtract_fusion.2
  59.7 0.0 copy-done.3
  59.8 0.0 copy-done.4
  59.8 0.9 multiply_add_fusion
  60.6 0.0 copy-start.2
  60.7 0.9 fusion.49
  61.6 0.0 copy-done.2
  61.6 0.9 fusion.15
  62.5 1.1 copy.21
  63.6 3.6 all-to-all-start.2
  67.2 0.9 fusion.40
  68.1 2.0 fusion.16
  70.2 0.0 copy-start.6
  70.2 1.1 copy.23
  71.2 5.3 %all-to-all-done.2 = bf16[64,4,768]{2,1,0:T(4,128)(2,1)S(1)} async-done(((bf16[64,4,768]{2,1,0:T(4,128)(2,1)}), bf16[64,4,768]{2,1,0:T(4,128)(2,1)S(1)}, u32[]{:S(2)}, u32[]{:S(2)}) %all-to-all-start.2) | async-done | bytes 393248 | tf_op jit(solution)/shard_map/all_to_all | solution.py:55
  76.5 3.6 all-to-all-start.3
  80.1 0.2 all-gather.2.cloned.1.call-start
  80.3 0.9 copy.42
  81.2 1.8 all_to_all.66
  83.0 6.4 %all-to-all-done.3 = bf16[64,4,768]{2,1,0:T(4,128)(2,1)S(1)} async-done(((bf16[64,4,768]{2,1,0:T(4,128)(2,1)}), bf16[64,4,768]{2,1,0:T(4,128)(2,1)S(1)}, u32[]{:S(2)}, u32[]{:S(2)}) %all-to-all-start.3) | async-done | bytes 393248 | tf_op jit(solution)/shard_map/all_to_all | solution.py:58
  89.4 0.1 copy.41
  89.6 0.8 all_to_all.70
  90.4 1.6 fusion.47
  92.0 0.0 copy-done.6
  92.0 1.8 fusion.121
  93.8 0.1 reduce_sum.43
  93.9 0.1 reduce_sum.45
  94.0 12.4 %all-reduce = (f32[256]{0:T(256)S(1)}, f32[256]{0:T(256)S(1)}) all-reduce(f32[256]{0:T(256)S(1)} %reduce_sum.45, f32[256]{0:T(256)S(1)} %reduce_sum.43), channel_id=1, replica_groups=mesh['row'=16,'col'=8] {'col'}, use_global_device_ids=true, to_apply=%region_7.8 | all-reduce | flops 512 | bytes 4096 | tf_op jit(solution)/shard_map/psum | solution.py:67
  106.4 0.9 fusion.25
  107.3 0.0 all-gather.2.cloned.1.call-update
  107.3 0.0 reduce-scatter.3.cloned.1.call-start
  107.4 56.5 %all-gather.2.cloned.1.call-done = bf16[4096,768]{1,0:T(8,128)(2,1)} async-done(((bf16[256,768]{1,0:T(8,128)(2,1)}), bf16[4096,768]{1,0:T(8,128)(2,1)}) %all-gather.2.cloned.1.call-update) | async-done | bytes 6291472 | tf_op jit(solution)/shard_map/all_gather | solution.py:70
  163.9 15.2 %convolution_convert_fusion = bf16[4096,1536]{1,0:T(8,128)(2,1)} fusion(bf16[4096,768]{1,0:T(8,128)(2,1)} %all-gather.2.cloned.1.call-done, bf16[768,1536]{1,0:T(8,128)(2,1)S(1)} %copy-done), kind=kOutput, calls=%fused_computation | convolution fusion | flops 9669967872 | bytes 21233664 | tf_op jit(solution)/shard_map/dot_general | solution.py:69
  179.1 0.0 reduce-scatter.3.cloned.1.call-update
  179.1 0.0 reduce-scatter.5.cloned.1.call-start
  179.2 72.0 %reduce-scatter.3.cloned.1.call-done = bf16[512,1536]{1,0:T(8,128)(2,1)} async-done(((bf16[4096,1536]{1,0:T(8,128)(2,1)}), bf16[512,1536]{1,0:T(8,128)(2,1)}) %reduce-scatter.3.cloned.1.call-update) | async-done | bytes 1572880 | tf_op jit(solution)/shard_map/reduce_scatter | solution.py:72
  251.2 8.1 %fusion.2 = bf16[512,1536]{1,0:T(8,128)(2,1)S(1)} fusion(bf16[512,1536]{1,0:T(8,128)(2,1)} %reduce-scatter.3.cloned.1.call-done, f32[1536]{0:T(1024)S(1)} %copy-done.7), kind=kLoop, calls=%fused_computation.5 | loop fusion | flops 52690944 | bytes 3151872 | tf_op jit(solution)/shard_map/convert_element_type | solution.py:75
  259.3 5.6 %stack.2 = bf16[8,512,1536]{2,1,0:T(8,128)(2,1)} broadcast(bf16[512,1536]{1,0:T(8,128)(2,1)S(1)} %fusion.2), dimensions={1,2} | broadcast | bytes 14155776 | tf_op jit(solution)/shard_map/stack | solution.py:78
  264.9 145.7 %all_to_all.77 = bf16[8,512,1536]{2,1,0:T(8,128)(2,1)S(1)} all-to-all(bf16[8,512,1536]{2,1,0:T(8,128)(2,1)} %stack.2), channel_id=1, replica_groups=mesh['row'=16,'col'=8] {'col'}, dimensions={0} | all-to-all | bytes 25165824 | tf_op jit(solution)/shard_map/all_to_all | solution.py:79
  410.6 11.7 %convolution_convert_fusion.1 = bf16[4096,768]{1,0:T(8,128)(2,1)} fusion(bf16[4096,1536]{1,0:T(8,128)(2,1)S(1)} %bitcast.99, bf16[1536,768]{1,0:T(8,128)(2,1)S(1)} %copy-done.10), kind=kOutput, calls=%fused_computation.1 | convolution fusion | flops 9666822144 | bytes 21233664 | tf_op jit(solution)/shard_map/dot_general | solution.py:83
  422.3 0.0 reduce-scatter.5.cloned.1.call-update
  422.3 81.0 %reduce-scatter.5.cloned.1.call-done = bf16[256,768]{1,0:T(8,128)(2,1)} async-done(((bf16[4096,768]{1,0:T(8,128)(2,1)}), bf16[256,768]{1,0:T(8,128)(2,1)}) %reduce-scatter.5.cloned.1.call-update) | async-done | bytes 393232 | tf_op jit(solution)/shard_map/reduce_scatter | solution.py:86
  503.3 1.9 fusion.27
  (16 shorter events, 0.1 us)
Async XLA Ops:
  6.5 157.3 %copy-start = (bf16[768,1536]{1,0:T(8,128)(2,1)S(1)}, bf16[768,1536]{1,0:T(8,128)(2,1)}, u32[]{:S(2)}) copy-start(bf16[768,1536]{1,0:T(8,128)(2,1)} %param.12) | copy-start | bytes 7077892
  6.5 27.1 %copy-start.5 = (bf16[4,64,768]{2,1,0:T(8,128)(2,1)S(1)}, bf16[4,64,768]{2,1,0:T(8,128)(2,1)}, u32[]{:S(2)}) copy-start(bf16[4,64,768]{2,1,0:T(8,128)(2,1)} %param.8) | copy-start | bytes 1179652
  6.5 27.1 %copy-start.11 = (f32[768]{0:T(1024)S(1)}, f32[768]{0:T(1024)}, u32[]{:S(2)}) copy-start(f32[768]{0:T(1024)} %param.10) | copy-start | bytes 9220
  25.6 17.4 %all-to-all-start.1 = ((bf16[4,64,768]{2,0,1:T(4,128)(2,1)}), bf16[4,64,768]{2,0,1:T(4,128)(2,1)S(1)}, u32[]{:S(2)}, u32[]{:S(2)}) async-start(bf16[4,64,768]{2,0,1:T(4,128)(2,1)} %copy.18), calls=%async_computation.1 | async-start | bytes 786432 | tf_op jit(solution)/shard_map/all_to_all | solution.py:36
  43.1 12.9 %all-to-all-start = ((bf16[4,64,768]{2,0,1:T(4,128)(2,1)}), bf16[4,64,768]{2,0,1:T(4,128)(2,1)S(1)}, u32[]{:S(2)}, u32[]{:S(2)}) async-start(bf16[4,64,768]{2,0,1:T(4,128)(2,1)} %copy.16), calls=%async_computation | async-start | bytes 786432 | tf_op jit(solution)/shard_map/all_to_all | solution.py:33
  58.0 1.8 copy-start.3
  58.0 1.8 copy-start.4
  60.6 0.9 copy-start.2
  63.6 12.9 %all-to-all-start.2 = ((bf16[64,4,768]{2,1,0:T(4,128)(2,1)}), bf16[64,4,768]{2,1,0:T(4,128)(2,1)S(1)}, u32[]{:S(2)}, u32[]{:S(2)}) async-start(bf16[64,4,768]{2,1,0:T(4,128)(2,1)} %copy.21), calls=%async_computation.2 | async-start | bytes 786432 | tf_op jit(solution)/shard_map/all_to_all | solution.py:55
  70.2 21.8 %copy-start.6 = (bf16[4,64,768]{2,1,0:T(8,128)(2,1)S(1)}, bf16[4,64,768]{2,1,0:T(8,128)(2,1)}, u32[]{:S(2)}) copy-start(bf16[4,64,768]{2,1,0:T(8,128)(2,1)} %param.8) | copy-start | bytes 1179652
  76.5 12.9 %all-to-all-start.3 = ((bf16[64,4,768]{2,1,0:T(4,128)(2,1)}), bf16[64,4,768]{2,1,0:T(4,128)(2,1)S(1)}, u32[]{:S(2)}, u32[]{:S(2)}) async-start(bf16[64,4,768]{2,1,0:T(4,128)(2,1)} %copy.23), calls=%async_computation.3 | async-start | bytes 786432 | tf_op jit(solution)/shard_map/all_to_all | solution.py:58
  80.1 83.8 %all-gather.2.cloned.1.call-start = ((), (), s32[]{:S(2)}) async-start(), calls=%async_computation.7 | async-start | bytes 6684672 | tf_op jit(solution)/shard_map/all_gather | solution.py:70
  81.2 25.2 %copy-start.8 = (f32[768]{0:T(1024)S(1)}, f32[768]{0:T(1024)}, u32[]{:S(2)}) copy-start(f32[768]{0:T(1024)} %param.11) | copy-start | bytes 9220
  107.3 143.9 %reduce-scatter.3.cloned.1.call-start = ((), (), s32[]{:S(2)}) async-start(), calls=%async_computation.8 | async-start | bytes 14155776 | tf_op jit(solution)/shard_map/reduce_scatter | solution.py:72
  179.1 72.1 %copy-start.7 = (f32[1536]{0:T(1024)S(1)}, f32[1536]{0:T(1024)}, u32[]{:S(2)}) copy-start(f32[1536]{0:T(1024)} %param.13) | copy-start | bytes 18436
  179.1 324.2 %reduce-scatter.5.cloned.1.call-start = ((), (), s32[]{:S(2)}) async-start(), calls=%async_computation.9 | async-start | bytes 6684672 | tf_op jit(solution)/shard_map/reduce_scatter | solution.py:86
  264.9 145.7 %copy-start.10 = (bf16[1536,768]{1,0:T(8,128)(2,1)S(1)}, bf16[1536,768]{1,0:T(8,128)(2,1)}, u32[]{:S(2)}) copy-start(bf16[1536,768]{1,0:T(8,128)(2,1)} %param.14) | copy-start | bytes 7077892
  422.3 82.9 %copy-start.1 = (bf16[768,1536]{1,0:T(8,128)(2,1)S(1)}, bf16[768,1536]{1,0:T(8,128)(2,1)}, u32[]{:S(2)}) copy-start(bf16[768,1536]{1,0:T(8,128)(2,1)} %param.12) | copy-start | bytes 7077892
  422.3 81.0 %copy-start.9 = (f32[768]{0:T(1024)S(1)}, f32[768]{0:T(1024)}, u32[]{:S(2)}) copy-start(f32[768]{0:T(1024)} %param.15) | copy-start | bytes 9220
Sparse Core Ops, SparseCore 0:
  107.5 56.3 all-gather.1
  179.3 71.9 reduce-scatter.2
  422.5 80.8 reduce-scatter.4
